TPU v7x, 32 devices: a whole 2x2x4 slice. The times are simulated.
32 devices in a mesh: groups: 2 (over y), dp: 4 (over x, core), tensor: 4 (over z).
Axes of the slice: x: 2, y: 2, z: 4, core: 2. Of those that a mesh axis runs over, the one named last changes fastest.
Arguments:
- attended: bfloat16 [512, 8192], P(('groups', 'dp'), 'tensor'), parts along dimension 0, may hold values from -6 to 6
- output_weight: bfloat16 [8192, 8192], P('tensor'), may hold values from -0.09375 to 0.09375
- down_factor_table: bfloat16 [32, 8192, 64], P('dp', 'tensor'), may hold values from -0.0625 to 0.0625
- up_factor_table: bfloat16 [32, 64, 8192], P('dp', None, 'tensor'), may hold values from -0.75 to 0.75
- request_adapter_index: int32 [512], P(('groups', 'dp')), parts along dimension 0, may hold values from 0 to 31, as said below
- adapter_row_table: int32 [64], P('groups'), parts along dimension 0, may hold values from 0 to 31, as said below
Outputs:
- projected: bfloat16 [512, 8192], P(('groups', 'dp'), 'tensor'), parts along dimension 0
There are 2 independent parts, one for each index of `groups`. A program takes and returns all parts, laid end to end along the dimension named above; an argument that names none is the same for every part. Nothing has to cross between parts.
Inputs may be any that keep to these rules, and one draw needn't show every extreme that they name: adapter_row_table is a permutation of the table rows. `request_adapter_index`: among the 64 requests of one index of dp, at most 32 have row_of in any one group of 8 consecutive table rows starting at a multiple of 8.
All inputs are finite; a program needn't handle non-finite values.
Results may differ from a plain program's by a relative error of at most 0.0075.
Values may be sent and summed in bfloat16 or wider, within the bound.
A program may use at most 128 MiB of HBM per device.

v0:
```python
import jax
import jax.numpy as jnp
from jax import lax
from jax.sharding import PartitionSpec as P


def local(
    attended,
    output_weight,
    down_factor_table,
    up_factor_table,
    request_adapter_index,
    adapter_row_table,
):
    table_len = adapter_row_table.shape[0]
    match = request_adapter_index[:, None] == jnp.arange(table_len, dtype=jnp.int32)[None, :]
    row_of = jnp.sum(jnp.where(match, adapter_row_table[None, :], 0), axis=1)
    partial_base = jnp.dot(attended, output_weight, preferred_element_type=jnp.float32)
    base = lax.psum_scatter(partial_base, "tensor", scatter_dimension=1, tiled=True)
    all_down, all_up = (
        lax.all_gather(down_factor_table, "dp", axis=0, tiled=True),
        lax.all_gather(up_factor_table, "dp", axis=0, tiled=True),
    )
    total = all_down.shape[0]
    projected_all = jnp.einsum(
        "rk,akj->raj", attended, all_down, preferred_element_type=jnp.float32
    )
    picker = (row_of[:, None] == jnp.arange(total, dtype=jnp.int32)[None, :]).astype(jnp.float32)
    low_part = jnp.einsum("raj,ra->rj", projected_all, picker)
    reduced_state = lax.psum(low_part, "tensor").astype(jnp.bfloat16)
    spread = picker.astype(jnp.bfloat16)[:, :, None] * reduced_state[:, None, :]
    delta = jnp.einsum("raj,ajk->rk", spread, all_up, preferred_element_type=jnp.float32)
    delta_half = lax.optimization_barrier(delta.astype(jnp.bfloat16))
    return (base + delta_half.astype(jnp.float32)).astype(jnp.bfloat16)


def solution(mesh):
    in_specs = (
        P(("groups", "dp"), "tensor"),
        P("tensor", None),
        P("dp", "tensor", None),
        P("dp", None, "tensor"),
        P(("groups", "dp")),
        P("groups"),
    )
    out_specs = P(("groups", "dp"), "tensor")
    return jax.shard_map(local, mesh=mesh, in_specs=in_specs, out_specs=out_specs, check_vma=False)
```

profile of v0, /device:TPU:0, one launch (start us, length us, event | category | flops | bytes accessed | tf_op | source)
XLA Modules:
  0.0 145.2 jit_solution(6965492720839332404)
XLA Ops:
  7.4 0.0 copy-start
  7.4 0.0 all-gather.3.cloned.1.call-start
  7.4 0.7 all-gather.3.cloned.1.call-update
  8.1 0.0 all-gather.5.cloned.1.call-start
  8.1 0.7 all-gather.5.cloned.1.call-update
  8.8 0.0 copy-start.1
  8.9 0.0 copy-start.2
  8.9 0.0 reduce-scatter.2.cloned.1.call-start
  8.9 0.0 copy-done
  8.9 15.4 %fusion.9 = f32[64,8192]{1,0:T(8,128)} fusion(bf16[64,2048]{1,0:T(8,128)(2,1)S(1)} %copy-done, bf16[2048,8192]{1,0:T(8,128)(2,1)} %param.7), kind=kOutput, calls=%fused_computation.15 | convolution fusion | flops 2147483648 | bytes 35913728 | tf_op jit(solution)/shard_map/dot_general | solution.py:18
  24.3 0.0 reduce-scatter.2.cloned.1.call-update
  24.3 0.0 copy-done.1
  24.3 0.0 copy-done.2
  24.3 0.1 select_reduce_fusion
  24.4 0.1 copy.8
  24.6 46.3 %all-gather.3.cloned.1.call-done = bf16[32,2048,64]{1,2,0:T(8,128)(2,1)} async-done(((bf16[8,2048,64]{1,2,0:T(8,128)(2,1)}), bf16[32,2048,64]{1,2,0:T(8,128)(2,1)}) %all-gather.3.cloned.1.call-update) | async-done | bytes 8388624 | tf_op jit(solution)/shard_map/all_gather | solution.py:21
  70.8 7.5 %fusion.4 = bf16[64,32,64]{2,0,1:T(8,128)(2,1)S(1)} fusion(bf16[32,2048,64]{1,2,0:T(8,128)(2,1)} %all-gather.3.cloned.1.call-done, bf16[64,2048]{1,0:T(8,128)(2,1)S(1)} %copy-done), kind=kOutput, calls=%fused_computation.6 | convolution fusion | flops 536870912 | bytes 8912896 | tf_op jit(solution)/shard_map/rk,akj->raj/dot_general | solution.py:25
  78.3 0.4 fusion.1
  78.8 19.0 %psum.7 = bf16[64,64]{1,0:T(8,128)(2,1)S(1)} all-reduce(f32[64,64]{1,0:T(8,128)S(1)} %bitcast.16), channel_id=1, replica_groups=mesh['groups'=2,'dp'=4,'tensor'=4] {'tensor'}, use_global_device_ids=true, to_apply=%region_2.3 | all-reduce | flops 4096 | bytes 24576 | tf_op jit(solution)/shard_map/psum | solution.py:30
  97.7 33.1 %all-gather.5.cloned.1.call-done = bf16[32,64,2048]{2,1,0:T(8,128)(2,1)} async-done(((bf16[8,64,2048]{2,1,0:T(8,128)(2,1)}), bf16[32,64,2048]{2,1,0:T(8,128)(2,1)}) %all-gather.5.cloned.1.call-update) | async-done | bytes 8388624 | tf_op jit(solution)/shard_map/all_gather | solution.py:22
  130.8 5.1 %fusion = bf16[64,2048]{1,0:T(8,128)(2,1)S(1)} fusion(bf16[32,64,2048]{2,1,0:T(8,128)(2,1)} %all-gather.5.cloned.1.call-done, bf16[64,64]{1,0:T(8,128)(2,1)S(1)} %psum.7, bf16[64,32]{0,1:T(8,128)(2,1)S(1)} %get-tuple-element.5), kind=kOutput, calls=%fused_computation.1 | convolution fusion | flops 537133056 | bytes 8663040 | tf_op jit(solution)/shard_map/raj,ajk->rk/dot_general | solution.py:32
  136.0 0.0 reduce-scatter.2.cloned.1.call-done
  136.0 1.8 %add_convert_fusion = bf16[64,2048]{1,0:T(8,128)(2,1)} fusion(f32[64,2048]{1,0:T(8,128)} %reduce-scatter.2.cloned.1.call-done, bf16[64,2048]{1,0:T(8,128)(2,1)S(1)} %fusion), kind=kLoop, calls=%fused_computation.4 | loop fusion | flops 393216 | bytes 1048576 | tf_op jit(solution)/shard_map/convert_element_type | solution.py:34
  (1 shorter events, 0.0 us)
Async XLA Ops:
  7.4 1.5 %copy-start = (bf16[64,2048]{1,0:T(8,128)(2,1)S(1)}, bf16[64,2048]{1,0:T(8,128)(2,1)}, u32[]{:S(2)}) copy-start(bf16[64,2048]{1,0:T(8,128)(2,1)} %param.6) | copy-start | bytes 786436
  7.4 63.5 %all-gather.3.cloned.1.call-start = ((), (), s32[]{:S(2)}) async-start(), calls=%async_computation.2 | async-start | bytes 10485760 | tf_op jit(solution)/shard_map/all_gather | solution.py:21
  8.1 122.7 %all-gather.5.cloned.1.call-start = ((), (), s32[]{:S(2)}) async-start(), calls=%async_computation.3 | async-start | bytes 10485760 | tf_op jit(solution)/shard_map/all_gather | solution.py:22
  8.8 15.5 %copy-start.1 = (s32[32]{0:T(128)S(1)}, s32[32]{0:T(128)}, u32[]{:S(2)}) copy-start(s32[32]{0:T(128)} %param.11) | copy-start | bytes 388
  8.9 15.5 %copy-start.2 = (s32[64]{0:T(128)S(1)}, s32[64]{0:T(128)}, u32[]{:S(2)}) copy-start(s32[64]{0:T(128)} %param.10) | copy-start | bytes 772
  8.9 127.1 %reduce-scatter.2.cloned.1.call-start = ((), (), s32[]{:S(2)}) async-start(), calls=%async_computation.1 | async-start | bytes 2621440 | tf_op jit(solution)/shard_map/reduce_scatter | solution.py:19
Sparse Core Ops, SparseCore 0:
  9.8 60.9 all-gather.2
  72.5 58.2 all-gather.4
Sparse Core Ops, SparseCore 1:
  24.4 46.9 reduce-scatter.1
where the time goes:
time: 145 us
  waiting for transfers between devices  80.8 us (56%)
  matrix products  28.4 us (20%)
  blocking collectives  19 us (13%)
  between operations  14.9 us (10%)
  other arithmetic  1.9 us (1%)
    all_gather x1, waiting for transfers between devices, local(): lax.all_gather(down_factor_table, 'dp', axis=0, tiled=True)  46.3 us
    all_gather x1, waiting for transfers between devices, local(): lax.all_gather(up_factor_table, 'dp', axis=0, tiled=True)  33.1 us
    psum x1, blocking collectives, local(): reduced_state = lax.psum(low_part, 'tensor').astype(jnp.bfloat16)  19 us
    dot_general x1, matrix products, local(): jnp.dot(attended, output_weight, preferred_element_type=jnp.float32)  15.4 us
    dot_general x1, matrix products, local(): jnp.einsum('rk,akj->raj', attended, all_down, preferred_element_type=jnp....  7.5 us
    dot_general x1, matrix products, local(): jnp.einsum('raj,ajk->rk', spread, all_up, preferred_element_type=jnp.floa...  5.14 us
  transfers between devices with their start and end apart: 3, of which 2 were waited for; matrix products, arithmetic and copies ran while one was open for 20% of the time, Pallas kernels for 0%

commit v1 on v0

v1 whole, which is shorter than its diff:
```python
import functools

import jax
import jax.numpy as jnp
from jax import lax
from jax.experimental import pallas as pl
from jax.experimental.pallas import tpu as pltpu
from jax.sharding import PartitionSpec as P

MESH = pl.DeviceIdType.MESH
F32, BF16 = jnp.float32, jnp.bfloat16


def kernel(
    n_dp, n_t, att_ref, sel_ref, loc_ref, w_ref, down_ref, up_ref, out_ref,
    wbuf, dbuf, ubuf, msg, msg_in, mask, low_own, low_in, dsend, din, ysend, yin, own,
    w_sem, ad_sem, msg_s, msg_r, low_s, low_r, d_s, d_r, y_s, y_r,
):
    d, t = lax.axis_index("dp"), lax.axis_index("tensor")
    depth = att_ref.shape[1]
    nch, chunk = wbuf.shape[1], wbuf.shape[3]
    width = nch * chunk
    cap = msg.shape[1]
    rows_c = n_dp * cap
    half = rows_c // 2
    lanes = low_own.shape[1]
    rank = lanes // 2
    spread_w = dbuf.shape[0]

    def block_at(s):
        down_b = jnp.where(n_t - 1 - s > t, n_t - 1 - s, n_t - 2 - s)
        up_b = jnp.where(s < t, s, s + 1)
        return jnp.where(s == n_t - 1, t, jnp.where(2 * t < n_t - 1, down_b, up_b))

    def w_copy(s, c):
        start = pl.multiple_of(block_at(s) * width + c * chunk, chunk)
        return pltpu.make_async_copy(
            w_ref.at[:, pl.ds(start, chunk)], wbuf.at[s, c], w_sem.at[s, c]
        )

    def fetch(s, _):
        for c in range(nch):
            w_copy(s, c).start()

    down_copy = pltpu.make_async_copy(down_ref, dbuf, ad_sem.at[0])
    up_copy = pltpu.make_async_copy(up_ref, ubuf, ad_sem.at[1])
    fetch(0, None)
    down_copy.start()
    lax.fori_loop(1, max(n_t // 2, 1), fetch, None)
    up_copy.start()
    lax.fori_loop(max(n_t // 2, 1), n_t, fetch, None)

    barrier = pltpu.get_barrier_semaphore()
    for j in range(1, n_dp):
        pl.semaphore_signal(
            barrier, inc=1, device_id={"dp": lax.rem(d + j, n_dp)}, device_id_type=MESH
        )
    for j in range(1, n_t):
        pl.semaphore_signal(
            barrier, inc=1, device_id={"tensor": lax.rem(t + j, n_t)}, device_id_type=MESH
        )
    rows_of = jnp.dot(sel_ref[...], att_ref[...], preferred_element_type=F32)
    msg[:, :, :depth] = rows_of.astype(BF16).reshape(n_dp, cap, depth)
    picks = jnp.dot(sel_ref[...], loc_ref[...], preferred_element_type=F32)
    msg[:, :, depth:] = picks.astype(BF16).reshape(n_dp, cap, lanes)
    msg_in[d] = msg[d]
    pl.semaphore_wait(barrier, n_dp - 1 + n_t - 1)

    def remote(src, dst, send, recv, axis, peer):
        return pltpu.make_async_remote_copy(
            src_ref=src, dst_ref=dst, send_sem=send, recv_sem=recv,
            device_id={axis: peer}, device_id_type=MESH,
        )

    def msg_copy(j):
        peer = lax.rem(d + j, n_dp)
        return remote(msg.at[peer], msg_in.at[d], msg_s.at[j], msg_r.at[d], "dp", peer)

    def msg_arrival(j):
        peer = lax.rem(d + j, n_dp)
        return remote(msg.at[peer], msg_in.at[peer], msg_s.at[j], msg_r.at[peer], "dp", peer)

    def low_copy(j):
        peer = lax.rem(t + j, n_t)
        return remote(low_own, low_in.at[t], low_s.at[j], low_r.at[t], "tensor", peer)

    def low_arrival(j):
        peer = lax.rem(t + j, n_t)
        return remote(low_own, low_in.at[peer], low_s.at[j], low_r.at[peer], "tensor", peer)

    def d_copy(j, c):
        peer = lax.rem(d + j, n_dp)
        return remote(
            dsend.at[peer, c], din.at[d, c], d_s.at[j, c], d_r.at[d, c], "dp", peer
        )

    def d_arrival(j, c):
        peer = lax.rem(d + j, n_dp)
        return remote(
            dsend.at[peer, c], din.at[peer, c], d_s.at[j, c], d_r.at[peer, c], "dp", peer
        )

    def y_copy(s, c):
        return remote(
            ysend.at[s, c], yin.at[t, c], y_s.at[s, c], y_r.at[t, c], "tensor", block_at(s)
        )

    def y_arrival(j, c):
        peer = lax.rem(t + j, n_t)
        return remote(
            ysend.at[0, c], yin.at[peer, c], y_s.at[0, c], y_r.at[peer, c], "tensor", peer
        )

    for j in range(n_dp - 1, 0, -1):
        msg_copy(j).start()

    def base_step(s, _):
        for c in range(nch):
            w_copy(s, c).wait()
            part = jnp.dot(att_ref[...], wbuf[s, c], preferred_element_type=F32)
            ysend[s, c] = part.astype(BF16)
            y_copy(s, c).start()

    first, second = (n_t - 1) // 2 + 1, n_t - 1
    first = min(first, second)
    lax.fori_loop(0, first, base_step, None)

    for j in range(1, n_dp):
        msg_arrival(j).wait_recv()
    down_copy.wait()
    got = msg_in[...].reshape(rows_c, depth + lanes)
    low = lax.dot_general(
        got[:, :depth], dbuf[...], (((1,), (1,)), ((), ())), preferred_element_type=F32
    )
    group = lax.broadcasted_iota(jnp.int32, (lanes, spread_w), 1) // rank
    index = lax.broadcasted_iota(jnp.int32, (lanes, spread_w), 0)
    expand = jnp.where(group == index, 1.0, 0.0).astype(BF16)
    mask[...] = jnp.dot(got[:, depth:], expand, preferred_element_type=F32)
    low = low * mask[...]
    folded = low[:, :lanes]
    for i in range(1, spread_w // lanes):
        folded = folded + low[:, i * lanes : (i + 1) * lanes]
    folded = folded + pltpu.roll(folded, rank, 1)
    left = lax.broadcasted_iota(jnp.int32, (half, lanes), 1) < rank
    low_own[...] = jnp.where(left, folded[:half], folded[half:])
    low_in[t] = low_own[...]
    for j in range(1, n_t):
        low_copy(j).start()

    lax.fori_loop(first, second, base_step, None)
    for c in range(nch):
        w_copy(n_t - 1, c).wait()
        own[c] = jnp.dot(att_ref[...], wbuf[n_t - 1, c], preferred_element_type=F32)

    for j in range(1, n_t):
        low_arrival(j).wait_recv()
    total = low_in[0]
    for i in range(1, n_t):
        total = total + low_in[i]
    turned = pltpu.roll(total, rank, 1)
    both = jnp.concatenate(
        [jnp.where(left, total, turned), jnp.where(left, turned, total)], axis=0
    )
    state = jnp.concatenate([both] * (spread_w // lanes), axis=1)
    spread = (state * mask[...]).astype(BF16)
    up_copy.wait()
    for c in range(nch):
        delta = jnp.dot(
            spread, ubuf[:, c * chunk : (c + 1) * chunk], preferred_element_type=F32
        )
        dsend[:, c] = delta.astype(BF16).reshape(n_dp, cap, chunk)
        din[d, c] = dsend[d, c]
        for j in range(n_dp - 1, 0, -1):
            d_copy(j, c).start()

    for c in range(nch):
        total = own[c]
        for j in range(1, n_t):
            y_arrival(j, c).wait_recv()
            total = total + yin[lax.rem(t + j, n_t), c].astype(F32)
        for j in range(1, n_dp):
            d_arrival(j, c).wait_recv()
        delta = lax.dot_general(
            sel_ref[...], din[:, c].reshape(rows_c, chunk), (((0,), (0,)), ((), ())),
            preferred_element_type=F32,
        )
        out_ref[:, c * chunk : (c + 1) * chunk] = (total + delta).astype(BF16)

    for j in range(1, n_dp):
        msg_copy(j).wait_send()
        for c in range(nch):
            d_copy(j, c).wait_send()
    for j in range(1, n_t):
        low_copy(j).wait_send()

    def drain(s, _):
        for c in range(nch):
            y_copy(s, c).wait_send()

    lax.fori_loop(0, n_t - 1, drain, None)


def local(
    n_dp, n_t, attended, output_weight, down_factor_table, up_factor_table,
    request_adapter_index, adapter_row_table,
):
    rows, depth = attended.shape
    adapters, _, rank = down_factor_table.shape
    columns = output_weight.shape[1] // n_t
    chunk = min(512, columns)
    nch = columns // chunk
    cap = 2 * rows // n_dp
    lanes = 2 * rank
    spread_w = adapters * rank

    table_len = adapter_row_table.shape[0]
    match = request_adapter_index[:, None] == jnp.arange(table_len, dtype=jnp.int32)[None, :]
    row_of = jnp.sum(jnp.where(match, adapter_row_table[None, :], 0), axis=1)
    owner, held = row_of // adapters, row_of % adapters
    earlier = jnp.arange(rows)[None, :] < jnp.arange(rows)[:, None]
    place = jnp.sum((owner[:, None] == owner[None, :]) & earlier, axis=1, dtype=jnp.int32)
    slot = owner * cap + place
    sel = (jnp.arange(n_dp * cap, dtype=jnp.int32)[:, None] == slot[None, :]).astype(BF16)
    loc = (held[:, None] == jnp.arange(lanes, dtype=jnp.int32)[None, :]).astype(BF16)
    down = jnp.swapaxes(down_factor_table, 1, 2).reshape(spread_w, depth)
    up = up_factor_table.reshape(spread_w, columns)

    vmem, anywhere = pl.BlockSpec(memory_space=pltpu.VMEM), pl.BlockSpec(memory_space=pl.ANY)
    dma = pltpu.SemaphoreType.DMA
    return pl.pallas_call(
        functools.partial(kernel, n_dp, n_t),
        out_shape=jax.ShapeDtypeStruct((rows, columns), BF16),
        in_specs=[vmem] * 3 + [anywhere] * 3,
        out_specs=vmem,
        scratch_shapes=[
            pltpu.VMEM((n_t, nch, depth, chunk), BF16),
            pltpu.VMEM((spread_w, depth), BF16),
            pltpu.VMEM((spread_w, columns), BF16),
            pltpu.VMEM((n_dp, cap, depth + lanes), BF16),
            pltpu.VMEM((n_dp, cap, depth + lanes), BF16),
            pltpu.VMEM((n_dp * cap, spread_w), F32),
            pltpu.VMEM((n_dp * cap // 2, lanes), F32),
            pltpu.VMEM((n_t, n_dp * cap // 2, lanes), F32),
            pltpu.VMEM((n_dp, nch, cap, chunk), BF16),
            pltpu.VMEM((n_dp, nch, cap, chunk), BF16),
            pltpu.VMEM((n_t, nch, rows, chunk), BF16),
            pltpu.VMEM((n_t, nch, rows, chunk), BF16),
            pltpu.VMEM((nch, rows, chunk), F32),
            dma((n_t, nch)),
            dma((2,)),
            dma((n_dp,)),
            dma((n_dp,)),
            dma((n_t,)),
            dma((n_t,)),
            dma((n_dp, nch)),
            dma((n_dp, nch)),
            dma((n_t, nch)),
            dma((n_t, nch)),
        ],
        compiler_params=pltpu.CompilerParams(
            collective_id=0, has_side_effects=True, vmem_limit_bytes=56 * 1024 * 1024
        ),
    )(attended, sel, loc, output_weight, down, up)


def solution(mesh):
    in_specs = (
        P(("groups", "dp"), "tensor"),
        P("tensor", None),
        P("dp", "tensor", None),
        P("dp", None, "tensor"),
        P(("groups", "dp")),
        P("groups"),
    )
    out_specs = P(("groups", "dp"), "tensor")
    body = functools.partial(local, mesh.shape["dp"], mesh.shape["tensor"])
    return jax.shard_map(body, mesh=mesh, in_specs=in_specs, out_specs=out_specs, check_vma=False)
```

time: 145 us -> 45.5 us (0.31)
  waiting for transfers between devices: 80.8 us -> 0 us
  Pallas kernels: 0 us -> 41.3 us
  matrix products: 28.4 us -> 0 us
  blocking collectives: 19 us -> 0 us
  between operations: 14.9 us -> 0.02 us
  local copies, waits for them, and re-layouts: 0.14 us -> 1.67 us
    all_gather x2 -> x0, waiting for transfers between devices: 79.3 us -> none  [the longest x1 46.3 us: local(): lax.all_gather(down_factor_table, 'dp', axis=0, tiled=True)]
    pallas_call x0 -> x1, Pallas kernels: none -> 41.3 us  [local(): pl.pallas_call(functools.partial(kernel, n_dp, n_t), out_shape=jax.ShapeD...]
    dot_general x4 -> x0, matrix products: 28.4 us -> none  [the longest x1 15.4 us: local(): jnp.dot(attended, output_weight, preferred_element_type=jnp.float32)]
    psum x1 -> x0, blocking collectives: 19 us -> none  [local(): reduced_state = lax.psum(low_part, 'tensor').astype(jnp.bfloat16)]
    unnamed x6 -> x1, local copies, waits for them, and re-layouts: 0.01 us -> 1.67 us
  transfers between devices with their start and end apart: 3 -> 0, of which waited for: 2 -> 0; matrix products, arithmetic and copies ran while one was open for 20% -> 0% of each run, Pallas kernels for 0% -> 0%
where the time goes in v1:
time: 45.5 us; the launch traced here: 45.3 us
  Pallas kernels  41.3 us (91%)
  other arithmetic  2.26 us (5%)
  local copies, waits for them, and re-layouts  1.67 us (4%)
    pallas_call x1, Pallas kernels, local(): pl.pallas_call(functools.partial(kernel, n_dp, n_t), out_shape=jax.ShapeD...  41.3 us
    unnamed x1, local copies, waits for them, and re-layouts  1.67 us

profile of v1, /device:TPU:0, one launch (start us, length us, event | category | flops | bytes accessed | tf_op | source)
XLA Modules:
  0.0 45.3 jit_solution(2550028039503329131)
XLA Ops:
  0.0 0.8 %select_reduce_fusion = s32[64]{0:T(128)S(1)} fusion(s32[32]{0:T(128)} %param.11, s32[64]{0:T(128)} %param.10), kind=kLoop, calls=%fused_computation.7 | loop fusion | flops 6080 | bytes 640 | tf_op jit(solution)/shard_map/reduce_sum | solution.py:218
  0.8 0.2 convert_reduce_fusion
  1.0 0.7 %fusion.2.loc_ref = bf16[64,128]{1,0:T(8,128)(2,1)} fusion(s32[64]{0:T(128)S(1)} %get-tuple-element.5), kind=kLoop, calls=%fused_computation.6 | loop fusion | flops 16384 | bytes 16640 | tf_op jit(solution)/shard_map/convert_element_type | solution.py:224
  1.6 0.6 %fusion.sel_ref = bf16[128,64]{1,0:T(8,128)(2,1)} fusion(s32[64]{0:T(128)S(1)} %multiply_add_fusion), kind=kLoop, calls=%fused_computation.1 | loop fusion | flops 16384 | bytes 16640 | tf_op jit(solution)/shard_map/convert_element_type | solution.py:223
  2.3 41.3 %shard_map.64 = bf16[64,2048]{1,0:T(8,128)(2,1)} custom-call(bf16[64,2048]{1,0:T(8,128)(2,1)} %att_ref.1, bf16[128,64]{1,0:T(8,128)(2,1)} %fusion.sel_ref, bf16[64,128]{1,0:T(8,128)(2,1)} %fusion.2.loc_ref, bf16[2048,8192]{1,0:T(8,128)(2,1)} %w_ref.1, bf16[512,2048]{1,0:T(8,128)(2,1)} %bitcast.4, bf16[512,2048]{1,0:T(8,128)(2,1)} %bitcast.5), custom_call_target="tpu_custom_call" | custom-call | tf_op jit(solution)/shard_map/pallas_call | solution.py:230
  43.6 1.7 %copy.8 = bf16[64,2048]{1,0:T(8,128)(2,1)} copy(bf16[64,2048]{1,0:T(8,128)(2,1)} %shard_map.64) | data formatting | bytes 524288
  (2 shorter events, 0.0 us)

commit v2 on v1

v2 whole, which is shorter than its diff:
```python
import functools

import jax
import jax.numpy as jnp
from jax import lax
from jax.experimental import pallas as pl
from jax.experimental.pallas import tpu as pltpu
from jax.sharding import PartitionSpec as P

MESH = pl.DeviceIdType.MESH
F32, BF16 = jnp.float32, jnp.bfloat16


def kernel(
    n_dp, n_t, adapters, att_hbm, idx_ref, tab_ref, w_ref, down_ref, up_ref, out_ref,
    att_ref, wbuf, dbuf, ubuf, sel_ref, msg, msg_in, mask, low_own, low_in, dsend, din,
    ysend, yin, own, w_sem, ad_sem, msg_s, msg_r, low_s, low_r, d_s, d_r, y_s, y_r,
):
    d, t = lax.axis_index("dp"), lax.axis_index("tensor")
    rows, depth = att_ref.shape
    nch, chunk = wbuf.shape[1], wbuf.shape[3]
    width = nch * chunk
    cap = msg.shape[1]
    rows_c = n_dp * cap
    half = rows_c // 2
    lanes = low_own.shape[1]
    rank = lanes // 2
    spread_w = dbuf.shape[0]
    steps = (n_t - 1) * nch
    edge = jnp.logical_or(t == 0, t == n_t - 1)

    barrier = pltpu.get_barrier_semaphore()
    for j in range(1, n_dp):
        pl.semaphore_signal(
            barrier, inc=1, device_id={"dp": lax.rem(d + j, n_dp)}, device_id_type=MESH
        )
    for j in range(1, n_t):
        pl.semaphore_signal(
            barrier, inc=1, device_id={"tensor": lax.rem(t + j, n_t)}, device_id_type=MESH
        )

    to_left, to_right = t, n_t - 1 - t
    shorter = jnp.minimum(to_left, to_right)
    right_longer = to_right >= to_left

    def block_at(s):
        in_turn = s < 2 * shorter
        k = jnp.where(in_turn, s // 2, s - shorter)
        even = lax.rem(s, 2) == 0
        right = jnp.logical_xor(jnp.logical_and(in_turn, jnp.logical_not(even)), right_longer)
        return jnp.where(s == n_t - 1, t, jnp.where(right, n_t - 1 - k, k))

    def w_copy(s, c):
        start = pl.multiple_of(block_at(s) * width + c * chunk, chunk)
        return pltpu.make_async_copy(
            w_ref.at[:, pl.ds(start, chunk)], wbuf.at[s, c], w_sem.at[s, c]
        )

    def fetch(s, _):
        for c in range(nch):
            w_copy(s, c).start()

    att_copy = pltpu.make_async_copy(att_hbm, att_ref, ad_sem.at[2])
    down_copy = pltpu.make_async_copy(down_ref, dbuf, ad_sem.at[0])
    up_copy = pltpu.make_async_copy(up_ref, ubuf, ad_sem.at[1])
    att_copy.start()
    early = max(n_t // 2, 1)
    fetch(0, None)
    down_copy.start()
    lax.fori_loop(1, early, fetch, None)
    up_copy.start()
    lax.fori_loop(early, n_t, fetch, None)

    @pl.when(t == 0)
    def _():
        yin[:n_t] = jnp.zeros((n_t,) + yin.shape[1:], BF16)

    @pl.when(t == n_t - 1)
    def _():
        yin[: n_t - 1] = jnp.zeros((n_t - 1,) + yin.shape[1:], BF16)
        yin[n_t] = jnp.zeros(yin.shape[1:], BF16)

    def iota(shape, axis):
        return lax.broadcasted_iota(jnp.int32, shape, axis)

    def flag(condition):
        return jnp.where(condition, 1.0, 0.0)

    table_len = tab_ref.shape[1]
    asked = flag(idx_ref[...] == iota((table_len, rows), 0)).astype(BF16)
    table = jnp.broadcast_to(tab_ref[...].astype(F32), (8, table_len)).astype(BF16)
    row_of = jnp.dot(table, asked, preferred_element_type=F32)[:1].astype(jnp.int32)
    group = iota((n_dp, rows), 0)
    owned = flag((row_of >= group * adapters) & (row_of < (group + 1) * adapters))
    earlier = flag(iota((rows, rows), 0) < iota((rows, rows), 1)).astype(BF16)
    place = jnp.dot(owned.astype(BF16), earlier, preferred_element_type=F32)
    group = group.astype(F32)
    slot = jnp.sum(owned * (group * cap + place), axis=0, keepdims=True).astype(jnp.int32)
    held = row_of - jnp.sum(owned * group * adapters, axis=0, keepdims=True).astype(jnp.int32)
    sel_ref[...] = flag(iota((rows_c, rows), 0) == slot).astype(BF16)
    held_at = flag(iota((lanes, rows), 0) == held).astype(BF16)
    picks = lax.dot_general(
        sel_ref[...], held_at, (((1,), (1,)), ((), ())), preferred_element_type=F32
    )
    msg[:, :, depth:] = picks.astype(BF16).reshape(n_dp, cap, lanes)
    att_copy.wait()
    rows_of = jnp.dot(sel_ref[...], att_ref[...], preferred_element_type=F32)
    msg[:, :, :depth] = rows_of.astype(BF16).reshape(n_dp, cap, depth)
    pl.semaphore_wait(barrier, n_dp - 1 + n_t - 1)

    def remote(src, dst, send, recv, axis, peer):
        return pltpu.make_async_remote_copy(
            src_ref=src, dst_ref=dst, send_sem=send, recv_sem=recv,
            device_id={axis: peer}, device_id_type=MESH,
        )

    def msg_copy(j):
        peer = lax.rem(d + j, n_dp)
        return remote(msg.at[peer], msg_in.at[d], msg_s.at[j], msg_r.at[d], "dp", peer)

    def msg_arrival(j):
        peer = lax.rem(d + j, n_dp)
        return remote(msg.at[peer], msg_in.at[peer], msg_s.at[j], msg_r.at[peer], "dp", peer)

    def low_copy(j):
        peer = lax.rem(t + j, n_t)
        return remote(low_own, low_in.at[t], low_s.at[j], low_r.at[t], "tensor", peer)

    def low_arrival(j):
        peer = lax.rem(t + j, n_t)
        return remote(low_own, low_in.at[peer], low_s.at[j], low_r.at[peer], "tensor", peer)

    def d_copy(j, c):
        peer = lax.rem(d + j, n_dp)
        return remote(
            dsend.at[peer, c], din.at[d, c], d_s.at[j, c], d_r.at[d, c], "dp", peer
        )

    def d_arrival(j, c):
        peer = lax.rem(d + j, n_dp)
        return remote(
            dsend.at[peer, c], din.at[peer, c], d_s.at[j, c], d_r.at[peer, c], "dp", peer
        )

    def y_copy(s, c):
        b = block_at(s)
        right = b > t
        peer = jnp.where(right, t + 1, t - 1)
        at = jnp.where(jnp.logical_and(b == peer, jnp.logical_not(right)), n_t, b)
        return remote(
            ysend.at[s, c], yin.at[at, c], y_s.at[s, c], y_r.at[at, c], "tensor", peer
        )

    def y_arrival(at, c):
        return remote(
            ysend.at[0, c], yin.at[at, c], y_s.at[0, c], y_r.at[at, c], "tensor",
            jnp.where(t > 0, t - 1, t + 1),
        )

    for j in range(n_dp - 1, 0, -1):
        msg_copy(j).start()
    msg_in[d] = msg[d]

    def base_step(q, _):
        s, c = q // nch, lax.rem(q, nch)
        w_copy(s, c).wait()
        part = jnp.dot(att_ref[...], wbuf[s, c], preferred_element_type=F32)
        b = block_at(s)

        @pl.when(jnp.logical_not(edge))
        def _():
            y_arrival(b, c).wait_recv()

        ysend[s, c] = (part + yin[b, c].astype(F32)).astype(BF16)
        y_copy(s, c).start()

    first = jnp.where(edge, max(steps // 2, 1), max((steps * 5) // 12, 1))
    lax.fori_loop(0, first, base_step, None)

    for j in range(1, n_dp):
        msg_arrival(j).wait_recv()
    down_copy.wait()
    got = msg_in[...].reshape(rows_c, depth + lanes)
    low = lax.dot_general(
        got[:, :depth], dbuf[...], (((1,), (1,)), ((), ())), preferred_element_type=F32
    )
    expand = flag(iota((lanes, spread_w), 1) // rank == iota((lanes, spread_w), 0)).astype(BF16)
    mask[...] = jnp.dot(got[:, depth:], expand, preferred_element_type=F32)
    low = low * mask[...]
    folded = low[:, :lanes]
    for i in range(1, spread_w // lanes):
        folded = folded + low[:, i * lanes : (i + 1) * lanes]
    folded = folded + pltpu.roll(folded, rank, 1)
    left = iota((half, lanes), 1) < rank
    low_own[...] = jnp.where(left, folded[:half], folded[half:]).astype(BF16)
    low_in[t] = low_own[...]
    for j in range(1, n_t):
        low_copy(j).start()

    lax.fori_loop(first, steps, base_step, None)
    for c in range(nch):
        w_copy(n_t - 1, c).wait()
        own[c] = jnp.dot(att_ref[...], wbuf[n_t - 1, c], preferred_element_type=F32)

    for j in range(1, n_t):
        low_arrival(j).wait_recv()
    total = low_in[0].astype(F32)
    for i in range(1, n_t):
        total = total + low_in[i].astype(F32)
    turned = pltpu.roll(total, rank, 1)
    both = jnp.concatenate(
        [jnp.where(left, total, turned), jnp.where(left, turned, total)], axis=0
    )
    state = jnp.concatenate([both] * (spread_w // lanes), axis=1)
    spread = (state * mask[...]).astype(BF16)
    up_copy.wait()
    for c in range(nch):
        delta = jnp.dot(
            spread, ubuf[:, c * chunk : (c + 1) * chunk], preferred_element_type=F32
        )
        dsend[:, c] = delta.astype(BF16).reshape(n_dp, cap, chunk)
        for j in range(n_dp - 1, 0, -1):
            d_copy(j, c).start()
        din[d, c] = dsend[d, c]

    for c in range(nch):
        @pl.when(t > 0)
        def _():
            y_arrival(t, c).wait_recv()

        @pl.when(t < n_t - 1)
        def _():
            y_arrival(n_t, c).wait_recv()

        base = own[c] + yin[t, c].astype(F32) + yin[n_t, c].astype(F32)
        for j in range(1, n_dp):
            d_arrival(j, c).wait_recv()
        delta = lax.dot_general(
            sel_ref[...], din[:, c].reshape(rows_c, chunk), (((0,), (0,)), ((), ())),
            preferred_element_type=F32,
        )
        out_ref[:, c * chunk : (c + 1) * chunk] = (base + delta).astype(BF16)

    for j in range(1, n_dp):
        msg_copy(j).wait_send()
        for c in range(nch):
            d_copy(j, c).wait_send()
    for j in range(1, n_t):
        low_copy(j).wait_send()

    def drain(s, _):
        for c in range(nch):
            y_copy(s, c).wait_send()

    lax.fori_loop(0, n_t - 1, drain, None)


def local(
    n_dp, n_t, attended, output_weight, down_factor_table, up_factor_table,
    request_adapter_index, adapter_row_table,
):
    rows, depth = attended.shape
    adapters, _, rank = down_factor_table.shape
    columns = output_weight.shape[1] // n_t
    chunk = min(512, columns)
    nch = columns // chunk
    cap = 2 * rows // n_dp
    lanes = 2 * rank
    spread_w = adapters * rank

    down = jnp.swapaxes(down_factor_table, 1, 2).reshape(spread_w, depth)
    up = up_factor_table.reshape(spread_w, columns)

    vmem, anywhere = pl.BlockSpec(memory_space=pltpu.VMEM), pl.BlockSpec(memory_space=pl.ANY)
    dma = pltpu.SemaphoreType.DMA
    return pl.pallas_call(
        functools.partial(kernel, n_dp, n_t, adapters),
        out_shape=jax.ShapeDtypeStruct((rows, columns), BF16),
        in_specs=[anywhere, vmem, vmem] + [anywhere] * 3,
        out_specs=vmem,
        scratch_shapes=[
            pltpu.VMEM((rows, depth), BF16),
            pltpu.VMEM((n_t, nch, depth, chunk), BF16),
            pltpu.VMEM((spread_w, depth), BF16),
            pltpu.VMEM((spread_w, columns), BF16),
            pltpu.VMEM((n_dp * cap, rows), BF16),
            pltpu.VMEM((n_dp, cap, depth + lanes), BF16),
            pltpu.VMEM((n_dp, cap, depth + lanes), BF16),
            pltpu.VMEM((n_dp * cap, spread_w), F32),
            pltpu.VMEM((n_dp * cap // 2, lanes), BF16),
            pltpu.VMEM((n_t, n_dp * cap // 2, lanes), BF16),
            pltpu.VMEM((n_dp, nch, cap, chunk), BF16),
            pltpu.VMEM((n_dp, nch, cap, chunk), BF16),
            pltpu.VMEM((n_t, nch, rows, chunk), BF16),
            pltpu.VMEM((n_t + 1, nch, rows, chunk), BF16),
            pltpu.VMEM((nch, rows, chunk), F32),
            dma((n_t, nch)),
            dma((3,)),
            dma((n_dp,)),
            dma((n_dp,)),
            dma((n_t,)),
            dma((n_t,)),
            dma((n_dp, nch)),
            dma((n_dp, nch)),
            dma((n_t, nch)),
            dma((n_t + 1, nch)),
        ],
        compiler_params=pltpu.CompilerParams(
            collective_id=0, has_side_effects=True, vmem_limit_bytes=56 * 1024 * 1024
        ),
    )(attended, request_adapter_index[None, :], adapter_row_table[None, :], output_weight, down, up)


def solution(mesh):
    in_specs = (
        P(("groups", "dp"), "tensor"),
        P("tensor", None),
        P("dp", "tensor", None),
        P("dp", None, "tensor"),
        P(("groups", "dp")),
        P("groups"),
    )
    out_specs = P(("groups", "dp"), "tensor")
    body = functools.partial(local, mesh.shape["dp"], mesh.shape["tensor"])
    return jax.shard_map(body, mesh=mesh, in_specs=in_specs, out_specs=out_specs, check_vma=False)
```

time: 45.5 us -> 32.9 us (0.72)
  the two profiles are of different devices: /device:TPU:0 before, /device:TPU:16 now
where the time goes in v2:
time: 32.9 us; the launch traced here: 32.7 us
  Pallas kernels  31.1 us (95%)
  local copies, waits for them, and re-layouts  1.67 us (5%)
    pallas_call x1, Pallas kernels, local(): pl.pallas_call(functools.partial(kernel, n_dp, n_t, adapters), out_shape=...  31.1 us
    unnamed x1, local copies, waits for them, and re-layouts  1.67 us

profile of v2, /device:TPU:16, one launch (start us, length us, event | category | flops | bytes accessed | tf_op | source)
XLA Modules:
  0.0 32.7 jit_solution(1566703585396213958)
XLA Ops:
  0.0 31.1 %shard_map.64 = bf16[64,2048]{1,0:T(8,128)(2,1)} custom-call(bf16[64,2048]{1,0:T(8,128)(2,1)} %att_hbm.1, s32[1,64]{1,0:T(1,128)} %bitcast.8, s32[1,32]{1,0:T(1,128)} %bitcast.9, bf16[2048,8192]{1,0:T(8,128)(2,1)} %w_ref.1, bf16[512,2048]{1,0:T(8,128)(2,1)} %bitcast.6, bf16[512,2048]{1,0:T(8,128)(2,1)} %bitcast.7), custom_call_target="tpu_custom_call" | custom-call | tf_op jit(solution)/shard_map/pallas_call | solution.py:276
  31.1 1.7 %copy.8 = bf16[64,2048]{1,0:T(8,128)(2,1)} copy(bf16[64,2048]{1,0:T(8,128)(2,1)} %shard_map.64) | data formatting | bytes 524288

commit v3 on v2

--- a/solution.py
+++ b/solution.py
@@ -56,20 +56,18 @@
             w_ref.at[:, pl.ds(start, chunk)], wbuf.at[s, c], w_sem.at[s, c]
         )
 
-    def fetch(s, _):
-        for c in range(nch):
-            w_copy(s, c).start()
+    ahead = min(3, n_t * nch)
+
+    def fetch(q):
+        w_copy(q // nch, lax.rem(q, nch)).start()
 
     att_copy = pltpu.make_async_copy(att_hbm, att_ref, ad_sem.at[2])
     down_copy = pltpu.make_async_copy(down_ref, dbuf, ad_sem.at[0])
     up_copy = pltpu.make_async_copy(up_ref, ubuf, ad_sem.at[1])
     att_copy.start()
-    early = max(n_t // 2, 1)
-    fetch(0, None)
+    for q in range(ahead):
+        fetch(jnp.int32(q))
     down_copy.start()
-    lax.fori_loop(1, early, fetch, None)
-    up_copy.start()
-    lax.fori_loop(early, n_t, fetch, None)
 
     @pl.when(t == 0)
     def _():
@@ -164,6 +162,11 @@
     def base_step(q, _):
         s, c = q // nch, lax.rem(q, nch)
         w_copy(s, c).wait()
+
+        @pl.when(q + ahead < n_t * nch)
+        def _():
+            fetch(q + ahead)
+
         part = jnp.dot(att_ref[...], wbuf[s, c], preferred_element_type=F32)
         b = block_at(s)
 
@@ -174,8 +177,10 @@
         ysend[s, c] = (part + yin[b, c].astype(F32)).astype(BF16)
         y_copy(s, c).start()
 
-    first = jnp.where(edge, max(steps // 2, 1), max((steps * 5) // 12, 1))
+    first = jnp.where(edge, max(steps * 6 // 12, 1), max(steps * 4 // 12, 1))
+    second = jnp.where(edge, max(steps * 10 // 12, 1), max(steps * 9 // 12, 1))
     lax.fori_loop(0, first, base_step, None)
+    up_copy.start()
 
     for j in range(1, n_dp):
         msg_arrival(j).wait_recv()
@@ -197,11 +202,7 @@
     for j in range(1, n_t):
         low_copy(j).start()
 
-    lax.fori_loop(first, steps, base_step, None)
-    for c in range(nch):
-        w_copy(n_t - 1, c).wait()
-        own[c] = jnp.dot(att_ref[...], wbuf[n_t - 1, c], preferred_element_type=F32)
-
+    lax.fori_loop(first, second, base_step, None)
     for j in range(1, n_t):
         low_arrival(j).wait_recv()
     total = low_in[0].astype(F32)
@@ -223,6 +224,13 @@
             d_copy(j, c).start()
         din[d, c] = dsend[d, c]
 
+    lax.fori_loop(second, steps, base_step, None)
+    for c in range(nch):
+        w_copy(n_t - 1, c).wait()
+        if steps + c + ahead < n_t * nch:
+            fetch(jnp.int32(steps + c + ahead))
+        own[c] = jnp.dot(att_ref[...], wbuf[n_t - 1, c], preferred_element_type=F32)
+
     for c in range(nch):
         @pl.when(t > 0)
         def _():
@@ -275,7 +283,7 @@
     dma = pltpu.SemaphoreType.DMA
     return pl.pallas_call(
         functools.partial(kernel, n_dp, n_t, adapters),
-        out_shape=jax.ShapeDtypeStruct((rows, columns), BF16),
+        out_shape=pltpu.VMEM((rows, columns), BF16),
         in_specs=[anywhere, vmem, vmem] + [anywhere] * 3,
         out_specs=vmem,
         scratch_shapes=[

time: 32.9 us -> 27.3 us (0.83)
  the two profiles are of different devices: /device:TPU:16 before, /device:TPU:0 now
where the time goes in v3:
time: 27.3 us; the launch traced here: 27.2 us
  Pallas kernels  26.4 us (97%)
  local copies, waits for them, and re-layouts  0.71 us (3%)
    pallas_call x1, Pallas kernels, local(): pl.pallas_call(functools.partial(kernel, n_dp, n_t, adapters), out_shape=...  26.4 us
    unnamed x1, local copies, waits for them, and re-layouts  0.71 us

profile of v3, /device:TPU:0, one launch (start us, length us, event | category | flops | bytes accessed | tf_op | source)
XLA Modules:
  0.0 27.2 jit_solution(4497075420516950618)
XLA Ops:
  0.0 26.4 %shard_map.64 = bf16[64,2048]{1,0:T(8,128)(2,1)S(1)} custom-call(bf16[64,2048]{1,0:T(8,128)(2,1)} %att_hbm.1, s32[1,64]{1,0:T(1,128)} %bitcast.8, s32[1,32]{1,0:T(1,128)} %bitcast.9, bf16[2048,8192]{1,0:T(8,128)(2,1)} %w_ref.1, bf16[512,2048]{1,0:T(8,128)(2,1)} %bitcast.6, bf16[512,2048]{1,0:T(8,128)(2,1)} %bitcast.7), custom_call_target="tpu_custom_call" | custom-call | tf_op jit(solution)/shard_map/pallas_call | solution.py:284
  26.5 0.7 %copy.8 = bf16[64,2048]{1,0:T(8,128)(2,1)} copy(bf16[64,2048]{1,0:T(8,128)(2,1)S(1)} %shard_map.64) | data formatting | bytes 524288

commit v4 on v3

--- a/solution.py
+++ b/solution.py
@@ -177,8 +177,8 @@
         ysend[s, c] = (part + yin[b, c].astype(F32)).astype(BF16)
         y_copy(s, c).start()
 
-    first = jnp.where(edge, max(steps * 6 // 12, 1), max(steps * 4 // 12, 1))
-    second = jnp.where(edge, max(steps * 10 // 12, 1), max(steps * 9 // 12, 1))
+    first = jnp.where(edge, max(steps * 6 // 12, 1), max(steps * 3 // 12, 1))
+    second = jnp.where(edge, max(steps * 10 // 12, 1), max(steps * 7 // 12, 1))
     lax.fori_loop(0, first, base_step, None)
     up_copy.start()
 

time: 27.3 us -> 26.8 us (0.982)
  Pallas kernels: 26.4 us -> 25.9 us
    pallas_call x1, Pallas kernels: 26.4 us -> 25.9 us  [local(): pl.pallas_call(functools.partial(kernel, n_dp, n_t, adapters), out_shape=...]
where the time goes in v4:
time: 26.8 us; the launch traced here: 26.6 us
  Pallas kernels  25.9 us (97%)
  local copies, waits for them, and re-layouts  0.71 us (3%)
    pallas_call x1, Pallas kernels, local(): pl.pallas_call(functools.partial(kernel, n_dp, n_t, adapters), out_shape=...  25.9 us
    unnamed x1, local copies, waits for them, and re-layouts  0.71 us

profile of v4, /device:TPU:0, one launch (start us, length us, event | category | flops | bytes accessed | tf_op | source)
XLA Modules:
  0.0 26.6 jit_solution(6223648064087118095)
XLA Ops:
  0.0 25.9 %shard_map.64 = bf16[64,2048]{1,0:T(8,128)(2,1)S(1)} custom-call(bf16[64,2048]{1,0:T(8,128)(2,1)} %att_hbm.1, s32[1,64]{1,0:T(1,128)} %bitcast.8, s32[1,32]{1,0:T(1,128)} %bitcast.9, bf16[2048,8192]{1,0:T(8,128)(2,1)} %w_ref.1, bf16[512,2048]{1,0:T(8,128)(2,1)} %bitcast.6, bf16[512,2048]{1,0:T(8,128)(2,1)} %bitcast.7), custom_call_target="tpu_custom_call" | custom-call | tf_op jit(solution)/shard_map/pallas_call | solution.py:284
  25.9 0.7 %copy.8 = bf16[64,2048]{1,0:T(8,128)(2,1)} copy(bf16[64,2048]{1,0:T(8,128)(2,1)S(1)} %shard_map.64) | data formatting | bytes 524288
